TPU v7x, 512 devices: a whole 4x4x16 slice. The times are simulated.
512 devices in a mesh: seq: 64 (over x, z), head: 8 (over y, core).
Axes of the slice: x: 4, y: 4, z: 16, core: 2. Of those that a mesh axis runs over, the one named last changes fastest.
Arguments:
- tokens: bfloat16 [16384, 5376], P('seq', 'head'), may hold values from -6 to 6
- features: bfloat16 [512, 64, 1152], P('seq'), may hold values from -6 to 6
- starts: int32 [8], replicated, may hold values from 0 to 16128, as said below
- sources: int32 [8], replicated, may hold values from 0 to 56, as said below
- soft_gain: float32 [1152], replicated, may hold values from 0.25 to 1.75
- proj_weight: bfloat16 [1152, 5376], P(None, 'head'), may hold values from -0.1875 to 0.1875
- input_gain: float32 [5376], replicated, may hold values from 0.25 to 1.75
- query_weight: bfloat16 [5376, 2048], P('seq', 'head'), may hold values from -0.078125 to 0.078125
- key_weight: bfloat16 [5376, 1024], P('seq', 'head'), may hold values from -0.078125 to 0.078125
- value_weight: bfloat16 [5376, 1024], P('seq', 'head'), may hold values from -0.078125 to 0.078125
- query_gain: float32 [128], replicated, may hold values from 0.25 to 1.75
- key_gain: float32 [128], replicated, may hold values from 0.25 to 1.75
- out_weight: bfloat16 [2048, 5376], P('seq', 'head'), may hold values from -0.125 to 0.125
- post_gain: float32 [5376], P('head'), may hold values from 0.25 to 1.75
Outputs:
- layer_out: bfloat16 [16384, 5376], P('seq', 'head')
Inputs may be any that keep to these rules, and one draw needn't show every extreme that they name: Image i takes positions starts[i] to starts[i] + 255; the spans are in increasing order of i, do not intersect, and each crosses one boundary between sequence shards. Distinct multiples of 8; image i's patches fill feature rows sources[i] * 8 onward.
All inputs are finite; a program needn't handle non-finite values.
Results may differ from a plain program's by a relative error of at most 0.012.
Values may be sent and summed in bfloat16 or wider, within the bound.
No kernel may reach another device: no remote copies, remote signals or barrier semaphores. Data moves between devices by JAX's collectives and lax.ppermute only.
A program may use at most 64 MiB of HBM per device.

v0:
```python
import jax
import jax.numpy as jnp
from jax import lax
from jax.sharding import Mesh
from jax.sharding import PartitionSpec as P

D = 5376
HEAD_DIM = 128
WINDOW = 1024
PATCH_SIDE = 64
POOL = 4
IMG_TOK = 256
SEQ = ("x", "z")
HEAD = ("y", "core")
EPSILON = 1e-06
QUERY_SCALE = 168.0 ** (-0.5)
ROPE_BASE = 10000.0


def shifted(value, axis, steps):
    count = lax.axis_size(axis)
    leading, last = (max(0, -steps), min(count, count - steps))
    return lax.ppermute(value, axis, [(source, source + steps) for source in range(leading, last)])


def rms_scale(inputs, scale_gain):
    return (
        inputs * lax.rsqrt(jnp.mean(inputs * inputs, axis=-1, keepdims=True) + EPSILON) * scale_gain
    )


def rotate(inputs, positions):
    half_dim = inputs.shape[-1] // 2
    frequency = ROPE_BASE ** (-jnp.arange(half_dim, dtype=jnp.float32) * 2.0 / inputs.shape[-1])
    angles = positions.astype(jnp.float32)[:, None] * frequency[None, :]
    cosine = jnp.cos(angles)[:, None, :]
    sine_part = jnp.sin(angles)[:, None, :]
    first_half = inputs[..., :half_dim]
    second = inputs[..., half_dim:]
    return jnp.concatenate(
        [first_half * cosine - second * sine_part, second * cosine + first_half * sine_part],
        axis=-1,
    )


def image_of(positions, starts):
    inside = (positions[:, None] >= starts[None, :]) & (
        positions[:, None] < starts[None, :] + IMG_TOK
    )
    labels = jnp.arange(1, starts.shape[0] + 1, dtype=jnp.int32)
    return jnp.sum(jnp.where(inside, labels[None, :], 0), axis=1) - 1


def allowed_keys(query_pos, key_pos, starts, total_rows):
    query_img = image_of(query_pos, starts)
    key_img = image_of(key_pos, starts)
    inside = (key_pos >= 0) & (key_pos < total_rows)
    in_window = query_pos[:, None] - key_pos[None, :] < WINDOW
    causal = key_pos[None, :] <= query_pos[:, None]
    same_image = (query_img[:, None] == key_img[None, :]) & (query_img[:, None] >= 0)
    return inside[None, :] & in_window & (causal | same_image)


def attend(queries, key_rows, values, allowed):
    scores = jnp.einsum("qgrd,kgd->grqk", queries, key_rows, preferred_element_type=jnp.float32)
    scores = jnp.where(allowed[None, None], scores, -jnp.inf)
    row_max = jnp.max(scores, axis=-1, keepdims=True)
    weights = jnp.exp(scores - row_max)
    row_sum = jnp.sum(weights, axis=-1)
    mixed_heads = jnp.einsum(
        "grqk,kgd->qgrd", weights.astype(jnp.bfloat16), values, preferred_element_type=jnp.float32
    )
    return (mixed_heads / jnp.transpose(row_sum, (2, 0, 1))[..., None]).astype(jnp.bfloat16)


def exchange(value, axes, count):
    spread = jnp.broadcast_to(value[None], (count, *value.shape))
    return lax.all_to_all(spread, axes, 0, 0, tiled=True)


def body(
    tokens,
    features,
    starts,
    sources,
    soft_gain,
    proj_weight,
    input_gain,
    query_weight,
    key_weight,
    value_weight,
    query_gain,
    key_gain,
    out_weight,
    post_gain,
):
    tok_rows, width = tokens.shape
    x_count = lax.axis_size("x")
    z_count = lax.axis_size("z")
    head_count = lax.axis_size("y") * lax.axis_size("core")
    seq_count = x_count * z_count
    x_index = lax.axis_index("x")
    z_index = lax.axis_index("z")
    head_index = lax.axis_index(HEAD)
    seq_index = lax.axis_index(SEQ)
    total_rows = seq_count * tok_rows
    rows_in = query_weight.shape[0]
    rows_out = out_weight.shape[0]
    qkv_local = jnp.concatenate([query_weight, key_weight, value_weight], axis=1)
    qkv_x = lax.all_gather(qkv_local, "x", axis=0, tiled=True)
    qkv_zx = lax.all_gather(qkv_x, "z", axis=0, tiled=True)
    out_x = lax.all_gather(out_weight, "x", axis=0, tiled=True)
    out_zx = lax.all_gather(out_x, "z", axis=0, tiled=True)
    image_count = starts.shape[0]
    vis = features.shape[2]
    pooled_side = PATCH_SIDE // POOL
    pool_rows = features.shape[0] // POOL
    block_rows = pool_rows * pooled_side
    shards_each = pooled_side // pool_rows
    patch_grid = features.reshape(pool_rows, POOL, pooled_side, POOL, vis)
    pooled = jnp.sum(patch_grid, axis=(1, 3), dtype=jnp.float32).reshape(block_rows, vis) / (
        POOL * POOL
    )
    soft = rms_scale(pooled, soft_gain).astype(jnp.bfloat16)
    vis_part = vis // head_count
    soft_part = lax.dynamic_slice_in_dim(soft, head_index * vis_part, vis_part, 1)
    soft_z = exchange(soft_part, "z", z_count).reshape(z_count * block_rows, vis_part)
    frame_pos = (
        (jnp.arange(x_count, dtype=jnp.int32)[:, None] * z_count + z_index) * tok_rows
        + jnp.arange(tok_rows, dtype=jnp.int32)[None, :]
    ).reshape(-1)
    frame_image = image_of(frame_pos, starts)
    row_base = sources // shards_each * (block_rows * shards_each) - starts
    image_ids = jnp.arange(image_count, dtype=jnp.int32)
    frame_row = jnp.sum(
        jnp.where(frame_image[:, None] == image_ids[None, :], row_base[None, :], 0), axis=1
    )
    frame_row = jnp.where(frame_image >= 0, frame_row + frame_pos, -1)
    here = x_index * (z_count * block_rows) + jnp.arange(z_count * block_rows, dtype=jnp.int32)
    chosen = (frame_row[:, None] == here[None, :]).astype(jnp.bfloat16)
    chosen = chosen.reshape(x_count, tok_rows, z_count * block_rows)
    frames = jnp.einsum("sk,xps->xkp", soft_z, chosen, preferred_element_type=jnp.float32)
    frames = lax.all_to_all(frames.astype(jnp.bfloat16), "x", 0, 0, tiled=True)
    mine = jnp.sum(frames.astype(jnp.float32), axis=0).astype(jnp.bfloat16)
    soft_rows = exchange(mine, HEAD, head_count).reshape(vis, tok_rows)
    embedded = lax.dot_general(
        soft_rows, proj_weight, (((0,), (0,)), ((), ())), preferred_element_type=jnp.float32
    ).astype(jnp.bfloat16)
    my_pos = seq_index * tok_rows + jnp.arange(tok_rows, dtype=jnp.int32)
    my_image = image_of(my_pos, starts)
    residual = jnp.where((my_image >= 0)[:, None], embedded, tokens)
    whole = exchange(residual, HEAD, head_count).astype(jnp.float32)
    mean_square = jnp.sum(whole * whole, axis=(0, 2), keepdims=True) / D
    gains = input_gain.reshape(head_count, 1, width)
    normed = (whole * lax.rsqrt(mean_square + EPSILON) * gains).astype(jnp.bfloat16)
    qkv_weight = (
        qkv_zx.reshape(z_count, x_count, rows_in, -1)
        .transpose(1, 0, 2, 3)
        .reshape(head_count, width, -1)
    )
    qkv = jnp.einsum("hqk,hkn->qn", normed, qkv_weight, preferred_element_type=jnp.float32)
    kv_local = key_weight.shape[1] // HEAD_DIM
    group_size = query_weight.shape[1] // key_weight.shape[1]
    q_width = query_weight.shape[1]
    k_width = key_weight.shape[1]
    query_sum = qkv[:, :q_width]
    key_sum = qkv[:, q_width : q_width + k_width]
    value_sum = qkv[:, q_width + k_width :]
    queries = (
        rotate(
            rms_scale(query_sum.reshape(tok_rows, kv_local * group_size, HEAD_DIM), query_gain),
            my_pos,
        )
        * QUERY_SCALE
    )
    queries = queries.astype(jnp.bfloat16).reshape(tok_rows, kv_local, group_size, HEAD_DIM)
    own_keys = (
        rotate(rms_scale(key_sum.reshape(tok_rows, kv_local, HEAD_DIM), key_gain), my_pos)
        .astype(jnp.bfloat16)
        .reshape(tok_rows, k_width)
    )
    own = jnp.concatenate([own_keys, value_sum.astype(jnp.bfloat16)], axis=1)
    past_count = WINDOW // tok_rows
    pieces = [shifted(own, SEQ, step) for step in range(past_count, 0, -1)]
    pieces += [own, shifted(own, SEQ, -1)]
    window = jnp.concatenate(pieces, axis=0)
    key_pos = (seq_index - past_count) * tok_rows + jnp.arange(window.shape[0], dtype=jnp.int32)
    allowed = allowed_keys(my_pos, key_pos, starts, total_rows)
    attended = attend(
        queries,
        window[:, :k_width].reshape(-1, kv_local, HEAD_DIM),
        window[:, k_width:].reshape(-1, kv_local, HEAD_DIM),
        allowed,
    )
    attended = attended.reshape(tok_rows, kv_local * group_size * HEAD_DIM)
    heads_all = exchange(attended, HEAD, head_count)
    heads_weight = (
        out_zx.reshape(z_count, x_count, rows_out, width)
        .transpose(1, 0, 2, 3)
        .reshape(head_count, q_width, width)
    )
    projected = jnp.einsum(
        "hqk,hkn->qn", heads_all, heads_weight, preferred_element_type=jnp.float32
    )
    squares = jnp.sum(exchange(jnp.sum(projected * projected, axis=1), HEAD, head_count), axis=0)
    post = projected * lax.rsqrt(squares[:, None] / D + EPSILON) * post_gain
    return (residual.astype(jnp.float32) + post).astype(jnp.bfloat16)


def solution(mesh):
    split = Mesh(mesh.devices.reshape(4, 16, 4, 2), ("x", "z", "y", "core"))
    return jax.shard_map(
        body,
        mesh=split,
        in_specs=(
            P(SEQ, HEAD),
            P(SEQ, None, None),
            P(),
            P(),
            P(),
            P(None, HEAD),
            P(),
            P(SEQ, HEAD),
            P(SEQ, HEAD),
            P(SEQ, HEAD),
            P(),
            P(),
            P(SEQ, HEAD),
            P(HEAD),
        ),
        out_specs=P(SEQ, HEAD),
        check_vma=False,
    )
```

profile of v0, /device:TPU:2, one launch (start us, length us, event | category | flops | bytes accessed | tf_op | source)
XLA Modules:
  0.0 253.8 jit_solution(5185182241604811078)
XLA Ops:
  6.5 0.9 maximum_bitcast_fusion
  7.5 15.1 %all-gather = bf16[4,84,512]{2,1,0:T(8,128)(2,1)S(1)} all-gather(bf16[1,84,512]{2,1,0:T(8,128)(2,1)S(1)} %maximum_bitcast_fusion), channel_id=1, replica_groups=mesh['x'=4,'z'=16,'y'=4,'core'=2] {'x'}, dimensions={0}, use_global_device_ids=true | all-gather | bytes 430080 | tf_op jit(solution)/shard_map/all_gather | solution.py:110
  22.6 0.8 reshape.474
  23.5 3.3 %reshape.472 = f32[2,4,16,4,1152]{4,3,2,1,0:T(4,128)} reshape(bf16[8,64,1152]{2,1,0:T(8,128)(2,1)} %param.15) | data formatting | bytes 3538944 | tf_op jit(solution)/shard_map/convert_element_type | solution.py:121
  26.8 2.2 reduce_sum.132
  29.2 0.8 dynamic-slice
  30.1 0.7 broadcast_in_dim.78
  30.8 12.8 %all-to-all-start = ((bf16[16,32,144]{2,1,0:T(8,128)(2,1)}), bf16[16,32,144]{2,1,0:T(8,128)(2,1)S(1)}, u32[]{:S(2)}, u32[]{:S(2)}) async-start(bf16[16,32,144]{2,1,0:T(8,128)(2,1)} %broadcast_in_dim.78), calls=%async_computation | async-start | bytes 524288 | tf_op jit(solution)/shard_map/all_to_all | solution.py:78
  44.1 18.5 %all-to-all-done = bf16[16,32,144]{2,1,0:T(8,128)(2,1)S(1)} async-done(((bf16[16,32,144]{2,1,0:T(8,128)(2,1)}), bf16[16,32,144]{2,1,0:T(8,128)(2,1)S(1)}, u32[]{:S(2)}, u32[]{:S(2)}) %all-to-all-start) | async-done | bytes 147488 | tf_op jit(solution)/shard_map/all_to_all | solution.py:78
  62.6 0.6 fusion.25
  63.2 9.7 %all_to_all.31 = bf16[4,144,256]{2,1,0:T(8,128)(2,1)S(1)} all-to-all(bf16[4,144,256]{2,1,0:T(8,128)(2,1)S(1)} %fusion.25), channel_id=1, replica_groups=mesh['x'=4,'z'=16,'y'=4,'core'=2] {'x'}, dimensions={0} | all-to-all | bytes 589824 | tf_op jit(solution)/shard_map/all_to_all | solution.py:143
  73.0 0.8 broadcast_in_dim.79
  73.8 4.7 %all-to-all-start.2 = ((bf16[8,144,256]{2,1,0:T(8,128)(2,1)}), bf16[8,144,256]{2,1,0:T(8,128)(2,1)S(1)}, u32[]{:S(2)}, u32[]{:S(2)}) async-start(bf16[8,144,256]{2,1,0:T(8,128)(2,1)} %broadcast_in_dim.79), calls=%async_computation.2 | async-start | bytes 1179648 | tf_op jit(solution)/shard_map/all_to_all | solution.py:78
  78.6 10.9 %all-to-all-done.2 = bf16[8,144,256]{2,1,0:T(8,128)(2,1)S(1)} async-done(((bf16[8,144,256]{2,1,0:T(8,128)(2,1)}), bf16[8,144,256]{2,1,0:T(8,128)(2,1)S(1)}, u32[]{:S(2)}, u32[]{:S(2)}) %all-to-all-start.2) | async-done | bytes 589856 | tf_op jit(solution)/shard_map/all_to_all | solution.py:78
  89.6 0.6 fusion.24
  90.2 1.7 broadcast_in_dim.80
  91.9 4.6 %all-to-all-start.3 = ((bf16[8,256,672]{1,2,0:T(8,128)(2,1)}), bf16[8,256,672]{1,2,0:T(8,128)(2,1)}, u32[]{:S(2)}, u32[]{:S(2)}) async-start(bf16[8,256,672]{1,2,0:T(8,128)(2,1)} %broadcast_in_dim.80), calls=%async_computation.3 | async-start | bytes 5505024 | tf_op jit(solution)/shard_map/all_to_all | solution.py:78
  96.6 12.3 %all_gather.14 = bf16[128,672]{1,0:T(8,128)(2,1)} all-gather(bf16[32,672]{1,0:T(8,128)(2,1)S(1)} %copy-done.1), channel_id=1, replica_groups=mesh['x'=4,'z'=16,'y'=4,'core'=2] {'x'}, dimensions={0}, use_global_device_ids=true | all-gather | bytes 215040 | tf_op jit(solution)/shard_map/all_gather | solution.py:112
  109.7 1.4 fusion.17
  111.1 19.6 %all-to-all-done.3 = bf16[8,256,672]{1,2,0:T(8,128)(2,1)} async-done(((bf16[8,256,672]{1,2,0:T(8,128)(2,1)}), bf16[8,256,672]{1,2,0:T(8,128)(2,1)}, u32[]{:S(2)}, u32[]{:S(2)}) %all-to-all-start.3) | async-done | bytes 2752544 | tf_op jit(solution)/shard_map/all_to_all | solution.py:78
  130.7 2.5 fusion
  133.3 8.9 %reshape.466 = bf16[16,4,84,512]{3,2,1,0:T(8,128)(2,1)} reshape(bf16[5376,512]{1,0:T(8,128)(2,1)} %all-gather.4.cloned.1.call-done) | data formatting | bytes 11010048 | tf_op jit(solution)/shard_map/reshape | solution.py:157
  142.2 5.7 %copy.56 = bf16[4,16,84,512]{3,2,1,0:T(8,128)(2,1)} copy(bf16[4,16,84,512]{3,2,0,1:T(8,128)(2,1)} %bitcast.76) | data formatting | bytes 11010048 | tf_op jit(solution)/shard_map/transpose | solution.py:158
  147.9 8.9 %reshape.467 = bf16[8,672,512]{2,1,0:T(8,128)(2,1)} reshape(bf16[4,16,84,512]{3,2,1,0:T(8,128)(2,1)} %copy.56) | data formatting | bytes 11010048 | tf_op jit(solution)/shard_map/reshape | solution.py:159
  156.8 6.6 %fusion.18 = f32[256,512]{1,0:T(8,128)S(1)} fusion(bf16[8,672,512]{2,1,0:T(8,128)(2,1)} %reshape.467, bf16[8,256,672]{1,2,0:T(8,128)(2,1)} %all-to-all-done.3, f32[8,672]{1,0:T(8,128)S(1)} %mul.255, f32[256]{0:T(256)S(1)} %add_rsqrt_fusion.3), kind=kOutput, calls=%fused_computation.22 | convolution fusion | flops 1414791168 | bytes 8804352 | tf_op jit(solution)/shard_map/hqk,hkn->qn/dot_general | solution.py:161
  164.4 4.9 %collective-permute-start = (bf16[256,256]{1,0:T(8,128)(2,1)S(1)}, bf16[256,256]{1,0:T(8,128)(2,1)}, u32[]{:S(2)}, u32[]{:S(2)}) collective-permute-start(bf16[256,256]{1,0:T(8,128)(2,1)S(1)} %pad_maximum_fusion), channel_id=1, source_target_pairs={{0,32},{8,40},{16,48},{24,56},{32,64},{40,72},{48,80},{56,88},{64,... | collective-permute-start | bytes 393224 | tf_op jit(solution)/shard_map/ppermute | solution.py:23
  169.3 3.5 %collective-permute-start.1 = (bf16[256,256]{1,0:T(8,128)(2,1)S(1)}, bf16[256,256]{1,0:T(8,128)(2,1)}, u32[]{:S(2)}, u32[]{:S(2)}) collective-permute-start(bf16[256,256]{1,0:T(8,128)(2,1)S(1)} %pad_maximum_fusion), channel_id=1, source_target_pairs={{0,24},{8,32},{16,40},{24,48},{32,56},{40,64},{48,72},{56,80},{64,... | collective-permute-start | bytes 393224 | tf_op jit(solution)/shard_map/ppermute | solution.py:23
  172.7 3.1 %collective-permute-start.2 = (bf16[256,256]{1,0:T(8,128)(2,1)S(1)}, bf16[256,256]{1,0:T(8,128)(2,1)}, u32[]{:S(2)}, u32[]{:S(2)}) collective-permute-start(bf16[256,256]{1,0:T(8,128)(2,1)S(1)} %pad_maximum_fusion), channel_id=1, source_target_pairs={{0,16},{8,24},{16,32},{24,40},{32,48},{40,56},{48,64},{56,72},{64,... | collective-permute-start | bytes 393224 | tf_op jit(solution)/shard_map/ppermute | solution.py:23
  175.9 4.1 %collective-permute-start.3 = (bf16[256,256]{1,0:T(8,128)(2,1)S(1)}, bf16[256,256]{1,0:T(8,128)(2,1)}, u32[]{:S(2)}, u32[]{:S(2)}) collective-permute-start(bf16[256,256]{1,0:T(8,128)(2,1)S(1)} %pad_maximum_fusion), channel_id=1, source_target_pairs={{0,8},{8,16},{16,24},{24,32},{32,40},{40,48},{48,56},{56,64},{64,7... | collective-permute-start | bytes 393224 | tf_op jit(solution)/shard_map/ppermute | solution.py:23
  180.0 4.0 %collective-permute-start.4 = (bf16[256,256]{1,0:T(8,128)(2,1)S(1)}, bf16[256,256]{1,0:T(8,128)(2,1)}, u32[]{:S(2)}, u32[]{:S(2)}) collective-permute-start(bf16[256,256]{1,0:T(8,128)(2,1)S(1)} %pad_maximum_fusion), channel_id=1, source_target_pairs={{8,0},{16,8},{24,16},{32,24},{40,32},{48,40},{56,48},{64,56},{72,6... | collective-permute-start | bytes 393224 | tf_op jit(solution)/shard_map/ppermute | solution.py:23
  185.0 2.0 collective-permute-done
  187.0 0.9 constant_dynamic-update-slice_fusion.5
  187.9 11.0 %collective-permute-done.1 = bf16[256,256]{1,0:T(8,128)(2,1)} collective-permute-done((bf16[256,256]{1,0:T(8,128)(2,1)S(1)}, bf16[256,256]{1,0:T(8,128)(2,1)}, u32[]{:S(2)}, u32[]{:S(2)}) %collective-permute-start.1) | collective-permute-done | bytes 131104 | tf_op jit(solution)/shard_map/ppermute | solution.py:23
  198.9 0.9 constant_dynamic-update-slice_fusion.4
  199.8 4.6 %collective-permute-done.2 = bf16[256,256]{1,0:T(8,128)(2,1)} collective-permute-done((bf16[256,256]{1,0:T(8,128)(2,1)S(1)}, bf16[256,256]{1,0:T(8,128)(2,1)}, u32[]{:S(2)}, u32[]{:S(2)}) %collective-permute-start.2) | collective-permute-done | bytes 131104 | tf_op jit(solution)/shard_map/ppermute | solution.py:23
  204.4 0.9 constant_dynamic-update-slice_fusion.3
  205.3 3.1 %collective-permute-done.3 = bf16[256,256]{1,0:T(8,128)(2,1)} collective-permute-done((bf16[256,256]{1,0:T(8,128)(2,1)S(1)}, bf16[256,256]{1,0:T(8,128)(2,1)}, u32[]{:S(2)}, u32[]{:S(2)}) %collective-permute-start.3) | collective-permute-done | bytes 131104 | tf_op jit(solution)/shard_map/ppermute | solution.py:23
  208.5 0.9 constant_dynamic-update-slice_fusion.2
  209.4 0.9 constant_dynamic-update-slice_fusion
  210.3 0.7 fusion.60
  211.5 0.7 fusion.34
  212.2 1.1 broadcast_in_dim.90
  213.3 3.9 %all-to-all-start.4 = ((bf16[8,256,256]{2,1,0:T(8,128)(2,1)}), bf16[8,256,256]{2,1,0:T(8,128)(2,1)S(1)}, u32[]{:S(2)}, u32[]{:S(2)}) async-start(bf16[8,256,256]{2,1,0:T(8,128)(2,1)} %broadcast_in_dim.90), calls=%async_computation.4 | async-start | bytes 2097152 | tf_op jit(solution)/shard_map/all_to_all | solution.py:78
  217.2 3.8 %copy.62 = bf16[16,4,32,672]{3,2,0,1:T(8,128)(2,1)} copy(bf16[16,4,32,672]{3,2,1,0:T(8,128)(2,1)} %bitcast.77) | data formatting | bytes 5505024 | tf_op jit(solution)/shard_map/reshape | solution.py:198
  221.0 12.1 %all-to-all-done.4 = bf16[8,256,256]{2,1,0:T(8,128)(2,1)S(1)} async-done(((bf16[8,256,256]{2,1,0:T(8,128)(2,1)}), bf16[8,256,256]{2,1,0:T(8,128)(2,1)S(1)}, u32[]{:S(2)}, u32[]{:S(2)}) %all-to-all-start.4) | async-done | bytes 1048608 | tf_op jit(solution)/shard_map/all_to_all | solution.py:78
  233.1 4.1 %multiply_reduce_fusion = (f32[256]{0:T(256)S(1)}, f32[256,672]{0,1:T(8,128)}) fusion(bf16[8,256,256]{2,1,0:T(8,128)(2,1)S(1)} %all-to-all-done.4, bf16[8,256,672]{2,1,0:T(8,128)(2,1)} %bitcast.78), kind=kOutput, calls=%fused_computation.33 | convolution fusion | flops 704986880 | bytes 4490240 | tf_op jit(solution)/shard_map/hqk,hkn->qn/dot_general | solution.py:202
  237.2 7.7 %all_to_all.32 = f32[8,1,256]{2,1,0:T(1,128)S(1)} all-to-all(f32[8,1,256]{2,1,0:T(1,128)S(1)} %broadcast_in_dim.91), channel_id=1, replica_groups=mesh['x'=4,'z'=16,'y'=4,'core'=2] {'y','core'}, dimensions={0} | all-to-all | bytes 16384 | tf_op jit(solution)/shard_map/all_to_all | solution.py:78
  244.9 2.0 add_convert_fusion
  (74 shorter events, 4.1 us)
Async XLA Ops:
  6.5 83.0 %copy-start = (bf16[1152,672]{0,1:T(8,128)(2,1)S(1)}, bf16[1152,672]{0,1:T(8,128)(2,1)}, u32[]{:S(2)}) copy-start(bf16[1152,672]{0,1:T(8,128)(2,1)} %param.19) | copy-start | bytes 4644868
  6.5 126.7 %all-gather.4.cloned.1.call-start = ((), (), s32[]{:S(2)}) async-start(), calls=%async_computation.6 | async-start | bytes 5849088 | tf_op jit(solution)/shard_map/all_gather | solution.py:111
  23.5 20.3 %copy-start.3 = (s32[8]{0:T(128)S(1)}, s32[8]{0:T(128)}, u32[]{:S(2)}) copy-start(s32[8]{0:T(128)} %param.16) | copy-start | bytes 100
  23.5 20.3 %copy-start.7 = (s32[8]{0:T(128)S(1)}, s32[8]{0:T(128)}, u32[]{:S(2)}) copy-start(s32[8]{0:T(128)} %param.17) | copy-start | bytes 100
  29.0 60.5 %copy-start.8 = (bf16[256,672]{0,1:T(8,128)(2,1)S(1)}, bf16[256,672]{0,1:T(8,128)(2,1)}, u32[]{:S(2)}) copy-start(bf16[256,672]{0,1:T(8,128)(2,1)} %param.14) | copy-start | bytes 1032196
  30.8 31.8 %all-to-all-start = ((bf16[16,32,144]{2,1,0:T(8,128)(2,1)}), bf16[16,32,144]{2,1,0:T(8,128)(2,1)S(1)}, u32[]{:S(2)}, u32[]{:S(2)}) async-start(bf16[16,32,144]{2,1,0:T(8,128)(2,1)} %broadcast_in_dim.78), calls=%async_computation | async-start | bytes 524288 | tf_op jit(solution)/shard_map/all_to_all | solution.py:78
  73.8 15.7 %all-to-all-start.2 = ((bf16[8,144,256]{2,1,0:T(8,128)(2,1)}), bf16[8,144,256]{2,1,0:T(8,128)(2,1)S(1)}, u32[]{:S(2)}, u32[]{:S(2)}) async-start(bf16[8,144,256]{2,1,0:T(8,128)(2,1)} %broadcast_in_dim.79), calls=%async_computation.2 | async-start | bytes 1179648 | tf_op jit(solution)/shard_map/all_to_all | solution.py:78
  91.9 4.6 %copy-start.1 = (bf16[32,672]{1,0:T(8,128)(2,1)S(1)}, bf16[32,672]{1,0:T(8,128)(2,1)}, u32[]{:S(2)}) copy-start(bf16[32,672]{1,0:T(8,128)(2,1)} %param.26) | copy-start | bytes 129028
  91.9 16.9 %copy-start.2 = (f32[5376]{0:T(1024)S(1)}, f32[5376]{0:T(1024)}, u32[]{:S(2)}) copy-start(f32[5376]{0:T(1024)} %param.20) | copy-start | bytes 64516
  91.9 38.8 %all-to-all-start.3 = ((bf16[8,256,672]{1,2,0:T(8,128)(2,1)}), bf16[8,256,672]{1,2,0:T(8,128)(2,1)}, u32[]{:S(2)}, u32[]{:S(2)}) async-start(bf16[8,256,672]{1,2,0:T(8,128)(2,1)} %broadcast_in_dim.80), calls=%async_computation.3 | async-start | bytes 5505024 | tf_op jit(solution)/shard_map/all_to_all | solution.py:78
  96.5 120.7 %all-gather.6.cloned.1.call-start = ((), (), s32[]{:S(2)}) async-start(), calls=%async_computation.7 | async-start | bytes 3342336 | tf_op jit(solution)/shard_map/all_gather | solution.py:113
  156.8 6.8 %copy-start.5 = (f32[128]{0:T(128)S(1)}, f32[128]{0:T(128)}, u32[]{:S(2)}) copy-start(f32[128]{0:T(128)} %param.25) | copy-start | bytes 1540
  156.8 27.8 %copy-start.6 = (f32[128]{0:T(128)S(1)}, f32[128]{0:T(128)}, u32[]{:S(2)}) copy-start(f32[128]{0:T(128)} %param.24) | copy-start | bytes 1540
  164.4 22.6 %collective-permute-start = (bf16[256,256]{1,0:T(8,128)(2,1)S(1)}, bf16[256,256]{1,0:T(8,128)(2,1)}, u32[]{:S(2)}, u32[]{:S(2)}) collective-permute-start(bf16[256,256]{1,0:T(8,128)(2,1)S(1)} %pad_maximum_fusion), channel_id=1, source_target_pairs={{0,32},{8,40},{16,48},{24,56},{32,64},{40,72},{48,80},{56,88},{64,... | collective-permute-start | bytes 393224 | tf_op jit(solution)/shard_map/ppermute | solution.py:23
  169.3 29.6 %collective-permute-start.1 = (bf16[256,256]{1,0:T(8,128)(2,1)S(1)}, bf16[256,256]{1,0:T(8,128)(2,1)}, u32[]{:S(2)}, u32[]{:S(2)}) collective-permute-start(bf16[256,256]{1,0:T(8,128)(2,1)S(1)} %pad_maximum_fusion), channel_id=1, source_target_pairs={{0,24},{8,32},{16,40},{24,48},{32,56},{40,64},{48,72},{56,80},{64,... | collective-permute-start | bytes 393224 | tf_op jit(solution)/shard_map/ppermute | solution.py:23
  172.7 31.7 %collective-permute-start.2 = (bf16[256,256]{1,0:T(8,128)(2,1)S(1)}, bf16[256,256]{1,0:T(8,128)(2,1)}, u32[]{:S(2)}, u32[]{:S(2)}) collective-permute-start(bf16[256,256]{1,0:T(8,128)(2,1)S(1)} %pad_maximum_fusion), channel_id=1, source_target_pairs={{0,16},{8,24},{16,32},{24,40},{32,48},{40,56},{48,64},{56,72},{64,... | collective-permute-start | bytes 393224 | tf_op jit(solution)/shard_map/ppermute | solution.py:23
  175.9 32.6 %collective-permute-start.3 = (bf16[256,256]{1,0:T(8,128)(2,1)S(1)}, bf16[256,256]{1,0:T(8,128)(2,1)}, u32[]{:S(2)}, u32[]{:S(2)}) collective-permute-start(bf16[256,256]{1,0:T(8,128)(2,1)S(1)} %pad_maximum_fusion), channel_id=1, source_target_pairs={{0,8},{8,16},{16,24},{24,32},{32,40},{40,48},{48,56},{56,64},{64,7... | collective-permute-start | bytes 393224 | tf_op jit(solution)/shard_map/ppermute | solution.py:23
  180.0 29.4 %collective-permute-start.4 = (bf16[256,256]{1,0:T(8,128)(2,1)S(1)}, bf16[256,256]{1,0:T(8,128)(2,1)}, u32[]{:S(2)}, u32[]{:S(2)}) collective-permute-start(bf16[256,256]{1,0:T(8,128)(2,1)S(1)} %pad_maximum_fusion), channel_id=1, source_target_pairs={{8,0},{16,8},{24,16},{32,24},{40,32},{48,40},{56,48},{64,56},{72,6... | collective-permute-start | bytes 393224 | tf_op jit(solution)/shard_map/ppermute | solution.py:23
  213.3 19.8 %all-to-all-start.4 = ((bf16[8,256,256]{2,1,0:T(8,128)(2,1)}), bf16[8,256,256]{2,1,0:T(8,128)(2,1)S(1)}, u32[]{:S(2)}, u32[]{:S(2)}) async-start(bf16[8,256,256]{2,1,0:T(8,128)(2,1)} %broadcast_in_dim.90), calls=%async_computation.4 | async-start | bytes 2097152 | tf_op jit(solution)/shard_map/all_to_all | solution.py:78
  221.0 23.9 %copy-start.4 = (f32[672]{0:T(1024)S(1)}, f32[672]{0:T(1024)}, u32[]{:S(2)}) copy-start(f32[672]{0:T(1024)} %param.27) | copy-start | bytes 8068
Sparse Core Ops, SparseCore 0:
  23.6 93.3 all-gather.3
  119.0 91.8 all-gather.5
where the time goes:
time: 255 us; the launch traced here: 254 us
  waiting for transfers between devices  82 us (32%)
  starting transfers between devices  45.6 us (18%)
  blocking collectives  44.8 us (18%)
  local copies, waits for them, and re-layouts  41.8 us (16%)
  between operations  13.8 us (5%)
  matrix products  13.3 us (5%)
  other arithmetic  12.5 us (5%)
    all_to_all x4, waiting for transfers between devices, exchange(): return lax.all_to_all(spread, axes, 0, 0, tiled=True)  61.2 us
    all_to_all x4, starting transfers between devices, exchange(): return lax.all_to_all(spread, axes, 0, 0, tiled=True)  25.9 us
    ppermute x5, waiting for transfers between devices, shifted(): lax.ppermute(value, axis, [(source, source + steps) for source in range(l...  20.7 us
    ppermute x5, starting transfers between devices, shifted(): lax.ppermute(value, axis, [(source, source + steps) for source in range(l...  19.6 us
    all_gather x1, blocking collectives, body(): qkv_x = lax.all_gather(qkv_local, 'x', axis=0, tiled=True)  15.1 us
    all_gather x1, blocking collectives, body(): out_x = lax.all_gather(out_weight, 'x', axis=0, tiled=True)  12.3 us
    all_to_all x1, blocking collectives, body(): frames = lax.all_to_all(frames.astype(jnp.bfloat16), 'x', 0, 0, tiled=True)  9.7 us
    reshape x1, local copies, waits for them, and re-layouts, body(): qkv_zx.reshape(z_count, x_count, rows_in, -1).transpose(1, 0, 2, 3)  8.91 us
  transfers between devices with their start and end apart: 11, of which 8 were waited for; matrix products, arithmetic and copies ran while one was open for 24% of the time, Pallas kernels for 0%

commit v1 on v0

--- a/solution.py
+++ b/solution.py
@@ -108,7 +108,8 @@
     rows_out = out_weight.shape[0]
     qkv_local = jnp.concatenate([query_weight, key_weight, value_weight], axis=1)
     qkv_x = lax.all_gather(qkv_local, "x", axis=0, tiled=True)
-    qkv_zx = lax.all_gather(qkv_x, "z", axis=0, tiled=True)
+    sent = jnp.stack([qkv_x] * lax.axis_size("z"))
+    qkv_zx = jnp.concatenate(lax.all_to_all(sent, "z", 0, 0), axis=0)
     out_x = lax.all_gather(out_weight, "x", axis=0, tiled=True)
     out_zx = lax.all_gather(out_x, "z", axis=0, tiled=True)
     image_count = starts.shape[0]

time: 255 us -> 505 us (1.98)
  waiting for transfers between devices: 82 us -> 324 us
  starting transfers between devices: 45.6 us -> 58.2 us
    all_to_all x0 -> x1, waiting for transfers between devices: none -> 253 us  [body(): qkv_zx = jnp.concatenate(lax.all_to_all(sent, 'z', 0, 0), axis=0)]
    ppermute x5, waiting for transfers between devices: 20.7 us -> 7.73 us  [shifted(): lax.ppermute(value, axis, [(source, source + steps) for source in range(l...]
    reshape x1 -> x0, local copies, waits for them, and re-layouts: 8.91 us -> none  [body(): qkv_zx.reshape(z_count, x_count, rows_in, -1).transpose(1, 0, 2, 3)]
    all_to_all x0 -> x1, starting transfers between devices: none -> 6.07 us  [body(): qkv_zx = jnp.concatenate(lax.all_to_all(sent, 'z', 0, 0), axis=0)]
    all_to_all x0 -> x1, local copies, waits for them, and re-layouts: none -> 5.65 us  [body(): qkv_zx = jnp.concatenate(lax.all_to_all(sent, 'z', 0, 0), axis=0)]
  transfers between devices with their start and end apart: 11 -> 11, of which waited for: 8 -> 8; matrix products, arithmetic and copies ran while one was open for 24% -> 9% of each run, Pallas kernels for 0% -> 0%
where the time goes in v1:
time: 505 us; the launch traced here: 504 us
  waiting for transfers between devices  324 us (64%)
  starting transfers between devices  58.2 us (12%)
  blocking collectives  42 us (8%)
  local copies, waits for them, and re-layouts  40.8 us (8%)
  between operations  13.9 us (3%)
  matrix products  13.2 us (3%)
  other arithmetic  11.6 us (2%)
    all_to_all x1, waiting for transfers between devices, body(): qkv_zx = jnp.concatenate(lax.all_to_all(sent, 'z', 0, 0), axis=0)  253 us
    all_to_all x4, waiting for transfers between devices, exchange(): return lax.all_to_all(spread, axes, 0, 0, tiled=True)  63.1 us
    all_to_all x4, starting transfers between devices, exchange(): return lax.all_to_all(spread, axes, 0, 0, tiled=True)  27.8 us
    ppermute x5, starting transfers between devices, shifted(): lax.ppermute(value, axis, [(source, source + steps) for source in range(l...  24.4 us
    all_gather x1, blocking collectives, body(): out_x = lax.all_gather(out_weight, 'x', axis=0, tiled=True)  12.4 us
    all_gather x1, blocking collectives, body(): qkv_x = lax.all_gather(qkv_local, 'x', axis=0, tiled=True)  11.9 us
  transfers between devices with their start and end apart: 11, of which 8 were waited for; matrix products, arithmetic and copies ran while one was open for 9% of the time, Pallas kernels for 0%

profile of v1, /device:TPU:2, one launch (start us, length us, event | category | flops | bytes accessed | tf_op | source)
XLA Modules:
  0.0 503.7 jit_solution(17134125720107044580)
XLA Ops:
  6.5 3.4 reshape.470
  9.9 2.2 reduce_sum.132
  12.4 0.8 dynamic-slice
  13.3 0.7 broadcast_in_dim.78
  14.0 15.2 %all-to-all-start = ((bf16[16,32,144]{2,1,0:T(8,128)(2,1)}), bf16[16,32,144]{2,1,0:T(8,128)(2,1)S(1)}, u32[]{:S(2)}, u32[]{:S(2)}) async-start(bf16[16,32,144]{2,1,0:T(8,128)(2,1)} %broadcast_in_dim.78), calls=%async_computation | async-start | bytes 524288 | tf_op jit(solution)/shard_map/all_to_all | solution.py:78
  29.6 17.9 %all-to-all-done = bf16[16,32,144]{2,1,0:T(8,128)(2,1)S(1)} async-done(((bf16[16,32,144]{2,1,0:T(8,128)(2,1)}), bf16[16,32,144]{2,1,0:T(8,128)(2,1)S(1)}, u32[]{:S(2)}, u32[]{:S(2)}) %all-to-all-start) | async-done | bytes 147488 | tf_op jit(solution)/shard_map/all_to_all | solution.py:78
  47.6 0.6 fusion.25
  48.2 10.0 %all_to_all.36 = bf16[4,144,256]{2,1,0:T(8,128)(2,1)S(1)} all-to-all(bf16[4,144,256]{2,1,0:T(8,128)(2,1)S(1)} %fusion.25), channel_id=1, replica_groups=mesh['x'=4,'z'=16,'y'=4,'core'=2] {'x'}, dimensions={0} | all-to-all | bytes 589824 | tf_op jit(solution)/shard_map/all_to_all | solution.py:144
  58.3 0.8 broadcast_in_dim.79
  59.1 4.5 all-to-all-start.2
  63.7 10.9 %all-to-all-done.2 = bf16[8,144,256]{2,1,0:T(8,128)(2,1)S(1)} async-done(((bf16[8,144,256]{2,1,0:T(8,128)(2,1)}), bf16[8,144,256]{2,1,0:T(8,128)(2,1)S(1)}, u32[]{:S(2)}, u32[]{:S(2)}) %all-to-all-start.2) | async-done | bytes 589856 | tf_op jit(solution)/shard_map/all_to_all | solution.py:78
  74.7 0.6 fusion.24
  75.3 1.7 broadcast_in_dim.80
  77.0 4.5 all-to-all-start.3
  81.6 11.9 %all-gather = bf16[4,84,512]{2,1,0:T(8,128)(2,1)S(1)} all-gather(bf16[1,84,512]{2,1,0:T(8,128)(2,1)S(1)} %maximum_bitcast_fusion), channel_id=1, replica_groups=mesh['x'=4,'z'=16,'y'=4,'core'=2] {'x'}, dimensions={0}, use_global_device_ids=true | all-gather | bytes 430080 | tf_op jit(solution)/shard_map/all_gather | solution.py:110
  93.6 22.2 %all-to-all-done.3 = bf16[8,256,672]{1,2,0:T(8,128)(2,1)} async-done(((bf16[8,256,672]{1,2,0:T(8,128)(2,1)}), bf16[8,256,672]{1,2,0:T(8,128)(2,1)}, u32[]{:S(2)}, u32[]{:S(2)}) %all-to-all-start.3) | async-done | bytes 2752544 | tf_op jit(solution)/shard_map/all_to_all | solution.py:78
  115.8 3.0 stack.2
  118.8 6.1 %all-to-all-start.4 = ((bf16[16,336,512]{2,1,0:T(8,128)(2,1)}), bf16[16,336,512]{2,1,0:T(8,128)(2,1)}, u32[]{:S(2)}, u32[]{:S(2)}) async-start(bf16[16,336,512]{2,1,0:T(8,128)(2,1)} %stack.2), calls=%async_computation.4 | async-start | bytes 11010048 | tf_op jit(solution)/shard_map/all_to_all | solution.py:112
  124.9 12.4 %all_gather.10 = bf16[128,672]{1,0:T(8,128)(2,1)} all-gather(bf16[32,672]{1,0:T(8,128)(2,1)S(1)} %copy-done.1), channel_id=1, replica_groups=mesh['x'=4,'z'=16,'y'=4,'core'=2] {'x'}, dimensions={0}, use_global_device_ids=true | all-gather | bytes 215040 | tf_op jit(solution)/shard_map/all_gather | solution.py:113
  138.2 1.4 fusion.17
  139.6 2.5 fusion
  142.2 253.0 %all-to-all-done.4 = bf16[16,336,512]{2,1,0:T(8,128)(2,1)} async-done(((bf16[16,336,512]{2,1,0:T(8,128)(2,1)}), bf16[16,336,512]{2,1,0:T(8,128)(2,1)}, u32[]{:S(2)}, u32[]{:S(2)}) %all-to-all-start.4) | async-done | bytes 5505056 | tf_op jit(solution)/shard_map/all_to_all | solution.py:112
  395.2 5.7 %copy.59 = bf16[16,336,512]{2,0,1:T(8,128)(2,1)S(1)} copy(bf16[16,336,512]{2,1,0:T(8,128)(2,1)} %all-to-all-done.4) | data formatting | bytes 11010048 | tf_op jit(solution)/shard_map/all_to_all | solution.py:112
  400.8 5.7 %copy.60 = bf16[4,16,84,512]{3,2,1,0:T(8,128)(2,1)} copy(bf16[4,16,84,512]{3,1,2,0:T(8,128)(2,1)S(1)} %bitcast.78) | data formatting | bytes 11010048 | tf_op jit(solution)/shard_map/transpose | solution.py:159
  406.5 8.9 %reshape.465 = bf16[8,672,512]{2,1,0:T(8,128)(2,1)} reshape(bf16[4,16,84,512]{3,2,1,0:T(8,128)(2,1)} %copy.60) | data formatting | bytes 11010048 | tf_op jit(solution)/shard_map/reshape | solution.py:160
  415.4 6.5 %fusion.18 = f32[256,512]{1,0:T(8,128)S(1)} fusion(bf16[8,672,512]{2,1,0:T(8,128)(2,1)} %reshape.465, bf16[8,256,672]{1,2,0:T(8,128)(2,1)} %all-to-all-done.3, f32[8,672]{1,0:T(8,128)S(1)} %mul.255, f32[256]{0:T(256)S(1)} %add_rsqrt_fusion.3), kind=kOutput, calls=%fused_computation.22 | convolution fusion | flops 1414791168 | bytes 8804352 | tf_op jit(solution)/shard_map/hqk,hkn->qn/dot_general | solution.py:162
  422.9 6.8 %collective-permute-start = (bf16[256,256]{1,0:T(8,128)(2,1)S(1)}, bf16[256,256]{1,0:T(8,128)(2,1)}, u32[]{:S(2)}, u32[]{:S(2)}) collective-permute-start(bf16[256,256]{1,0:T(8,128)(2,1)S(1)} %pad_maximum_fusion), channel_id=1, source_target_pairs={{0,32},{8,40},{16,48},{24,56},{32,64},{40,72},{48,80},{56,88},{64,... | collective-permute-start | bytes 393224 | tf_op jit(solution)/shard_map/ppermute | solution.py:23
  429.7 6.2 %collective-permute-start.1 = (bf16[256,256]{1,0:T(8,128)(2,1)S(1)}, bf16[256,256]{1,0:T(8,128)(2,1)}, u32[]{:S(2)}, u32[]{:S(2)}) collective-permute-start(bf16[256,256]{1,0:T(8,128)(2,1)S(1)} %pad_maximum_fusion), channel_id=1, source_target_pairs={{0,24},{8,32},{16,40},{24,48},{32,56},{40,64},{48,72},{56,80},{64,... | collective-permute-start | bytes 393224 | tf_op jit(solution)/shard_map/ppermute | solution.py:23
  435.9 3.2 collective-permute-start.2
  439.1 3.6 collective-permute-start.3
  442.7 4.5 collective-permute-start.4
  448.3 0.9 constant_dynamic-update-slice_fusion.5
  449.2 2.3 collective-permute-done.1
  451.4 0.9 constant_dynamic-update-slice_fusion.4
  452.3 3.9 collective-permute-done.2
  456.2 0.9 constant_dynamic-update-slice_fusion.3
  457.1 1.6 collective-permute-done.3
  458.7 0.9 constant_dynamic-update-slice_fusion.2
  459.7 0.9 constant_dynamic-update-slice_fusion
  460.6 0.7 fusion.60
  461.7 0.7 fusion.34
  462.5 1.1 broadcast_in_dim.90
  463.6 3.6 all-to-all-start.5
  467.2 3.8 copy.66
  471.0 12.0 %all-to-all-done.5 = bf16[8,256,256]{2,1,0:T(8,128)(2,1)S(1)} async-done(((bf16[8,256,256]{2,1,0:T(8,128)(2,1)}), bf16[8,256,256]{2,1,0:T(8,128)(2,1)S(1)}, u32[]{:S(2)}, u32[]{:S(2)}) %all-to-all-start.5) | async-done | bytes 1048608 | tf_op jit(solution)/shard_map/all_to_all | solution.py:78
  483.0 4.1 multiply_reduce_fusion
  487.1 7.7 %all_to_all.37 = f32[8,1,256]{2,1,0:T(1,128)S(1)} all-to-all(f32[8,1,256]{2,1,0:T(1,128)S(1)} %broadcast_in_dim.91), channel_id=1, replica_groups=mesh['x'=4,'z'=16,'y'=4,'core'=2] {'y','core'}, dimensions={0} | all-to-all | bytes 16384 | tf_op jit(solution)/shard_map/all_to_all | solution.py:78
  494.8 2.0 add_convert_fusion
  (80 shorter events, 4.1 us)
Async XLA Ops:
  6.5 68.1 %copy-start = (bf16[1152,672]{0,1:T(8,128)(2,1)S(1)}, bf16[1152,672]{0,1:T(8,128)(2,1)}, u32[]{:S(2)}) copy-start(bf16[1152,672]{0,1:T(8,128)(2,1)} %param.19) | copy-start | bytes 4644868
  6.5 22.8 %copy-start.6 = (s32[8]{0:T(128)S(1)}, s32[8]{0:T(128)}, u32[]{:S(2)}) copy-start(s32[8]{0:T(128)} %param.16) | copy-start | bytes 100
  6.5 22.8 %copy-start.10 = (s32[8]{0:T(128)S(1)}, s32[8]{0:T(128)}, u32[]{:S(2)}) copy-start(s32[8]{0:T(128)} %param.17) | copy-start | bytes 100
  12.2 62.5 %copy-start.11 = (bf16[256,672]{0,1:T(8,128)(2,1)S(1)}, bf16[256,672]{0,1:T(8,128)(2,1)}, u32[]{:S(2)}) copy-start(bf16[256,672]{0,1:T(8,128)(2,1)} %param.14) | copy-start | bytes 1032196
  14.0 33.6 %all-to-all-start = ((bf16[16,32,144]{2,1,0:T(8,128)(2,1)}), bf16[16,32,144]{2,1,0:T(8,128)(2,1)S(1)}, u32[]{:S(2)}, u32[]{:S(2)}) async-start(bf16[16,32,144]{2,1,0:T(8,128)(2,1)} %broadcast_in_dim.78), calls=%async_computation | async-start | bytes 524288 | tf_op jit(solution)/shard_map/all_to_all | solution.py:78
  59.1 15.5 %all-to-all-start.2 = ((bf16[8,144,256]{2,1,0:T(8,128)(2,1)}), bf16[8,144,256]{2,1,0:T(8,128)(2,1)S(1)}, u32[]{:S(2)}, u32[]{:S(2)}) async-start(bf16[8,144,256]{2,1,0:T(8,128)(2,1)} %broadcast_in_dim.79), calls=%async_computation.2 | async-start | bytes 1179648 | tf_op jit(solution)/shard_map/all_to_all | solution.py:78
  77.0 4.6 copy-start.2
  77.0 4.6 copy-start.4
  77.0 4.6 copy-start.5
  77.0 38.8 %all-to-all-start.3 = ((bf16[8,256,672]{1,2,0:T(8,128)(2,1)}), bf16[8,256,672]{1,2,0:T(8,128)(2,1)}, u32[]{:S(2)}, u32[]{:S(2)}) async-start(bf16[8,256,672]{1,2,0:T(8,128)(2,1)} %broadcast_in_dim.80), calls=%async_computation.3 | async-start | bytes 5505024 | tf_op jit(solution)/shard_map/all_to_all | solution.py:78
  118.8 6.1 %copy-start.1 = (bf16[32,672]{1,0:T(8,128)(2,1)S(1)}, bf16[32,672]{1,0:T(8,128)(2,1)}, u32[]{:S(2)}) copy-start(bf16[32,672]{1,0:T(8,128)(2,1)} %param.26) | copy-start | bytes 129028
  118.8 18.6 %copy-start.3 = (f32[5376]{0:T(1024)S(1)}, f32[5376]{0:T(1024)}, u32[]{:S(2)}) copy-start(f32[5376]{0:T(1024)} %param.20) | copy-start | bytes 64516
  118.8 276.4 %all-to-all-start.4 = ((bf16[16,336,512]{2,1,0:T(8,128)(2,1)}), bf16[16,336,512]{2,1,0:T(8,128)(2,1)}, u32[]{:S(2)}, u32[]{:S(2)}) async-start(bf16[16,336,512]{2,1,0:T(8,128)(2,1)} %stack.2), calls=%async_computation.4 | async-start | bytes 11010048 | tf_op jit(solution)/shard_map/all_to_all | solution.py:112
  124.9 342.3 %all-gather.3.cloned.1.call-start = ((), (), s32[]{:S(2)}) async-start(), calls=%async_computation.7 | async-start | bytes 3342336 | tf_op jit(solution)/shard_map/all_gather | solution.py:114
  415.4 6.7 %copy-start.8 = (f32[128]{0:T(128)S(1)}, f32[128]{0:T(128)}, u32[]{:S(2)}) copy-start(f32[128]{0:T(128)} %param.25) | copy-start | bytes 1540
  415.4 32.6 %copy-start.9 = (f32[128]{0:T(128)S(1)}, f32[128]{0:T(128)}, u32[]{:S(2)}) copy-start(f32[128]{0:T(128)} %param.24) | copy-start | bytes 1540
  422.9 25.4 %collective-permute-start = (bf16[256,256]{1,0:T(8,128)(2,1)S(1)}, bf16[256,256]{1,0:T(8,128)(2,1)}, u32[]{:S(2)}, u32[]{:S(2)}) collective-permute-start(bf16[256,256]{1,0:T(8,128)(2,1)S(1)} %pad_maximum_fusion), channel_id=1, source_target_pairs={{0,32},{8,40},{16,48},{24,56},{32,64},{40,72},{48,80},{56,88},{64,... | collective-permute-start | bytes 393224 | tf_op jit(solution)/shard_map/ppermute | solution.py:23
  429.7 21.7 %collective-permute-start.1 = (bf16[256,256]{1,0:T(8,128)(2,1)S(1)}, bf16[256,256]{1,0:T(8,128)(2,1)}, u32[]{:S(2)}, u32[]{:S(2)}) collective-permute-start(bf16[256,256]{1,0:T(8,128)(2,1)S(1)} %pad_maximum_fusion), channel_id=1, source_target_pairs={{0,24},{8,32},{16,40},{24,48},{32,56},{40,64},{48,72},{56,80},{64,... | collective-permute-start | bytes 393224 | tf_op jit(solution)/shard_map/ppermute | solution.py:23
  435.9 20.3 %collective-permute-start.2 = (bf16[256,256]{1,0:T(8,128)(2,1)S(1)}, bf16[256,256]{1,0:T(8,128)(2,1)}, u32[]{:S(2)}, u32[]{:S(2)}) collective-permute-start(bf16[256,256]{1,0:T(8,128)(2,1)S(1)} %pad_maximum_fusion), channel_id=1, source_target_pairs={{0,16},{8,24},{16,32},{24,40},{32,48},{40,56},{48,64},{56,72},{64,... | collective-permute-start | bytes 393224 | tf_op jit(solution)/shard_map/ppermute | solution.py:23
  439.1 19.6 %collective-permute-start.3 = (bf16[256,256]{1,0:T(8,128)(2,1)S(1)}, bf16[256,256]{1,0:T(8,128)(2,1)}, u32[]{:S(2)}, u32[]{:S(2)}) collective-permute-start(bf16[256,256]{1,0:T(8,128)(2,1)S(1)} %pad_maximum_fusion), channel_id=1, source_target_pairs={{0,8},{8,16},{16,24},{24,32},{32,40},{40,48},{48,56},{56,64},{64,7... | collective-permute-start | bytes 393224 | tf_op jit(solution)/shard_map/ppermute | solution.py:23
  442.7 16.9 %collective-permute-start.4 = (bf16[256,256]{1,0:T(8,128)(2,1)S(1)}, bf16[256,256]{1,0:T(8,128)(2,1)}, u32[]{:S(2)}, u32[]{:S(2)}) collective-permute-start(bf16[256,256]{1,0:T(8,128)(2,1)S(1)} %pad_maximum_fusion), channel_id=1, source_target_pairs={{8,0},{16,8},{24,16},{32,24},{40,32},{48,40},{56,48},{64,56},{72,6... | collective-permute-start | bytes 393224 | tf_op jit(solution)/shard_map/ppermute | solution.py:23
  463.6 19.4 %all-to-all-start.5 = ((bf16[8,256,256]{2,1,0:T(8,128)(2,1)}), bf16[8,256,256]{2,1,0:T(8,128)(2,1)S(1)}, u32[]{:S(2)}, u32[]{:S(2)}) async-start(bf16[8,256,256]{2,1,0:T(8,128)(2,1)} %broadcast_in_dim.90), calls=%async_computation.5 | async-start | bytes 2097152 | tf_op jit(solution)/shard_map/all_to_all | solution.py:78
  471.0 23.8 %copy-start.7 = (f32[672]{0:T(1024)S(1)}, f32[672]{0:T(1024)}, u32[]{:S(2)}) copy-start(f32[672]{0:T(1024)} %param.27) | copy-start | bytes 8068
Sparse Core Ops, SparseCore 0:
  137.5 248.6 all-gather.2
